TPU v7x, 128 devices: a whole 4x4x4 slice. The times are simulated.
128 devices in a mesh: col: 8 (over z, core), row: 16 (over x, y).
Axes of the slice: x: 4, y: 4, z: 4, core: 2. Of those that a mesh axis runs over, the one named last changes fastest.
Arguments:
- affinity: bfloat16 [15360, 128, 128], P(('col', 'row')), may hold values from 0 to 0.015625
- tile_rows: int32 [15360], P(('col', 'row')), may hold values from 0 to 39
- tile_cols: int32 [15360], P(('col', 'row')), may hold values from 0 to 79
- live_tiles: int32 [128], P(('col', 'row')), may hold values from 1 to 120, as said below
- start: float32 [81920, 256], P(('col', 'row')), may hold values from -1500 to 1500
Outputs:
- vectors: float32 [81920, 256], P(('col', 'row'))
- first_passes: float32 [2, 81920, 256], P(None, ('col', 'row'))
Inputs may be any that keep to these rules, and one draw needn't show every extreme that they name: A device's tiles are its slots 0 to live_tiles - 1; later slots are ignored. Some device holds exactly 120 tiles.
All inputs are finite; a program needn't handle non-finite values.
Results may differ from a plain program's by a relative error of at most 0.0003.
Values sent between devices are 32-bit elements; how exact they have to be, the bound alone decides.
A program may use at most 128 MiB of HBM per device.

v0:
```python
import jax
import jax.numpy as jnp
from jax import lax
from jax.sharding import Mesh
from jax.sharding import PartitionSpec as P

ITERS = 2
ROW = ("row_0", "row_1")
COL = ("col_0", "col_1")
COL_ROW = ("col_0", "col_1", "row_0", "row_1")
highest = lax.Precision.HIGHEST


def cut_along(value, dim, devices):
    before, after = (value.shape[:dim], value.shape[dim + 1 :])
    return jnp.moveaxis(value.reshape(*before, devices, -1, *after), dim, 0)


def sent_and_summed(value, axis, dim):
    parts = cut_along(value, dim, lax.axis_size(axis))
    arrived = lax.all_to_all(parts, axis, split_axis=0, concat_axis=0, tiled=True)
    return arrived.sum(axis=0)


def sum_in_two_steps(value, axes, dim):
    far, near = axes
    parts = cut_along(value, dim, lax.axis_size(far))
    nearer = sent_and_summed(parts, near, dim + 1)
    arrived = lax.all_to_all(nearer, far, split_axis=0, concat_axis=0, tiled=True)
    return arrived.sum(axis=0)


def rows_for(lines, devices):
    spare = -lines.shape[0] % devices
    if not spare:
        return lines
    return jnp.concatenate([lines, jnp.zeros((spare, *lines.shape[1:]), lines.dtype)])


def sent_to_all(value, axis):
    copies = jnp.broadcast_to(value, (lax.axis_size(axis), *value.shape))
    return lax.all_to_all(copies, axis, split_axis=0, concat_axis=0, tiled=True)


def joined_along(parts, dim):
    lengths = list(parts.shape[1:])
    lengths[dim] *= parts.shape[0]
    return jnp.moveaxis(parts, 0, dim).reshape(lengths)


def whole_of(value, axes, dim):
    far, near = axes
    initial = sent_to_all(value, far)
    parts = jnp.swapaxes(sent_to_all(initial, near), 0, 1)
    return joined_along(parts.reshape(-1, *value.shape), dim)


def nested_sum(value, axes):
    lines = value.reshape(-1, value.shape[-1])
    own = sum_in_two_steps(
        rows_for(lines, lax.axis_size(axes[0]) * lax.axis_size(axes[1])), axes, 0
    )
    whole = whole_of(own, axes, 0)
    return whole[: len(lines)].reshape(value.shape)


def total_of(value, axes):
    own = sum_in_two_steps(
        rows_for(value, lax.axis_size(axes[0]) * lax.axis_size(axes[1])), axes, 0
    )
    whole = whole_of(own, axes, 0)
    return whole[: len(value)].reshape(value.shape)


def together(arrays, axis):
    ends = [0]
    for a in arrays:
        ends.append(ends[-1] + a.size)
    subtotal = total_of(jnp.concatenate([a.ravel() for a in arrays]), axis)
    return tuple((subtotal[b:e].reshape(a.shape) for a, b, e in zip(arrays, ends, ends[1:])))


def local_gram(matrix):
    return jnp.dot(matrix.T, matrix, precision=highest, preferred_element_type=jnp.float32)


def inverse_lower(gram):
    lower = jnp.linalg.cholesky(gram)
    return jax.scipy.linalg.solve_triangular(
        lower, jnp.eye(gram.shape[0], dtype=jnp.float32), lower=True
    )


def apply_factor(matrix, inverse):
    return jnp.dot(matrix, inverse.T, precision=highest, preferred_element_type=jnp.float32)


def body(affinity, tile_rows, tile_cols, live_tiles, start):
    n_row = lax.axis_size(ROW)
    n_col = lax.axis_size(COL)
    slot_count = affinity.shape[0]
    tile_size = affinity.shape[1]
    rows_local = start.shape[0]
    vec_count = start.shape[1]
    own_tiles = rows_local // tile_size
    live = (jnp.arange(slot_count) < live_tiles[0]).astype(jnp.float32)
    row_onehot = (jnp.arange(own_tiles * n_col)[:, None] == tile_rows[None, :]).astype(
        jnp.float32
    ) * live[None, :]
    row_sums = jnp.sum(affinity, axis=2, dtype=jnp.float32)
    degree_terms = jnp.dot(
        row_onehot, row_sums, precision=highest, preferred_element_type=jnp.float32
    )
    degree = 1.0 + sent_and_summed(degree_terms, COL, 0).reshape(rows_local)
    scaling = (1.0 / jnp.sqrt(degree))[:, None]
    squares = affinity.astype(jnp.float32)
    firsts = []
    pending = start
    for step_number in range(ITERS):
        mapped_scaled = scaling * pending
        gathered = lax.all_gather(mapped_scaled, ROW, axis=0, tiled=True)
        gathered = gathered.reshape(n_row * own_tiles, tile_size, vec_count)
        picked = gathered[tile_cols]
        products = jnp.einsum(
            "sij,sjk->sik", squares, picked, precision=highest, preferred_element_type=jnp.float32
        )
        terms = jnp.dot(
            row_onehot,
            products.reshape(slot_count, tile_size * vec_count),
            precision=highest,
            preferred_element_type=jnp.float32,
        )
        summed = sum_in_two_steps(terms, ("col_0", "col_1"), 0)
        raw_image = scaling * (mapped_scaled + summed.reshape(rows_local, vec_count))
        if step_number == 0:
            inner_gram = nested_sum(local_gram(raw_image), (("col_0", "col_1", "row_0"), "row_1"))
            image_block = raw_image
        else:
            raw_gram, pending_gram = together(
                (local_gram(raw_image), local_gram(pending)), (("col_0", "col_1", "row_0"), "row_1")
            )
            pending_inverse = inverse_lower(pending_gram)
            image_block = apply_factor(raw_image, pending_inverse)
            inner_gram = jnp.dot(
                jnp.dot(
                    pending_inverse, raw_gram, precision=highest, preferred_element_type=jnp.float32
                ),
                pending_inverse.T,
                precision=highest,
                preferred_element_type=jnp.float32,
            )
        pending = apply_factor(image_block, inverse_lower(inner_gram))
        firsts.append(pending)
    final_gram = nested_sum(local_gram(pending), (("col_0", "col_1", "row_0"), "row_1"))
    basis = apply_factor(pending, inverse_lower(final_gram))
    total_images = rows_local * n_row * n_col
    root = jnp.sqrt(jnp.float32(total_images))
    return (root * basis, root * jnp.stack(firsts, axis=0))


def solution(mesh):
    torus = Mesh(mesh.devices.reshape(4, 2, 4, 4), ("col_0", "col_1", "row_0", "row_1"))
    return jax.shard_map(
        body,
        mesh=torus,
        in_specs=(P(COL_ROW, None, None), P(COL_ROW), P(COL_ROW), P(COL_ROW), P(COL_ROW, None)),
        out_specs=(P(COL_ROW, None), P(None, COL_ROW, None)),
        check_vma=False,
    )
```

profile of v0, /device:TPU:0, one launch (start us, length us, event | category | flops | bytes accessed | tf_op | source)
XLA Modules:
  0.0 914.5 jit_solution(9744506423480880370)
XLA Ops:
  26.3 79.2 %all-gather.3.cloned.1.call-done = f32[10240,256]{1,0:T(8,128)} async-done(((f32[640,256]{1,0:T(8,128)}), f32[10240,256]{1,0:T(8,128)}) %all-gather.3.cloned.1.call-update) | async-done | bytes 10485776 | tf_op jit(solution)/shard_map/all_gather | solution.py:121
  105.5 13.6 %gather_fusion = f32[120,128,256]{2,1,0:T(8,128)} fusion(f32[80,128,256]{2,1,0:T(8,128)} %bitcast.176, s32[1024]{0:T(1024)S(1)} %pad_clamp_fusion), kind=kCustom, calls=%fused_computation | custom fusion | bytes 31457760 | tf_op jit(solution)/shard_map/gather | solution.py:123
  119.1 20.2 %convolution_bitcast_fusion.3 = f32[120,128,256]{1,2,0:T(8,128)} fusion(f32[120,128,256]{2,1,0:T(8,128)} %gather_fusion, bf16[120,128,128]{2,1,0:T(8,128)(2,1)} %param.8), kind=kOutput, calls=%fused_computation.15 | convolution fusion | flops 6039797760 | bytes 35389440 | tf_op jit(solution)/shard_map/sij,sjk->sik/dot_general | solution.py:124
  139.3 15.6 %copy.101 = f32[120,128,256]{2,1,0:T(8,128)} copy(f32[120,128,256]{1,2,0:T(8,128)} %convolution_bitcast_fusion.3) | data formatting | bytes 31457280 | tf_op jit(solution)/shard_map/sij,sjk->sik/dot_general | solution.py:124
  154.9 17.9 %reshape.193 = f32[120,32768,1,1]{1,0,2,3:T(8,128)} reshape(f32[120,128,256]{2,1,0:T(8,128)} %copy.101) | data formatting | bytes 31457280 | tf_op jit(solution)/shard_map/reshape | solution.py:129
  172.8 16.1 %convolution_bitcast_fusion.1 = f32[2,4,5,32768]{3,2,0,1:T(8,128)S(1)} fusion(f32[120,32768,1,1]{1,0,2,3:T(8,128)} %reshape.193, f32[120]{0:T(128)S(1)} %compare_convert_fusion, s32[120]{0:T(128)S(1)} %copy-done.1, s32[4,2,5]{2,1,0:T(2,128)S(1)} %multiply_add_fusion), kind=kOutput, calls=%fused_computation.11 | convolution fusion | flops 1887446400 | bytes 20972640 | tf_op jit(solution)/shard_map/dot_general | solution.py:127
  207.5 63.5 %all_to_all.97 = f32[4,5,32768]{2,1,0:T(8,128)} all-to-all(f32[4,5,32768]{2,1,0:T(8,128)S(1)} %copy.103), channel_id=1, replica_groups=mesh['col_0'=4,'col_1'=2,'row_0'=4,'row_1'=4] {'col_0'}, dimensions={0} | all-to-all | bytes 5242880 | tf_op jit(solution)/shard_map/all_to_all | solution.py:29
  343.2 11.7 %cholesky.231 = f32[128,128]{1,0:T(8,128)S(1)} custom-call(f32[128,128]{1,0:T(8,128)S(1)} %convolution_subtract_fusion.7), custom_call_target="Cholesky" | custom-call | tf_op jit(solution)/shard_map/jit(cholesky)/cholesky | solution.py:88
  362.2 19.7 %custom-call.18 = f32[2,128,128]{1,2,0:T(8,128)S(1)} custom-call(f32[2,128,128]{2,1,0:T(8,128)S(1)} %get-tuple-element.30), custom_call_target="InvertDiagBlocksLowerTriangular" | custom-call | tf_op jit(solution)/shard_map/jit(_solve_triangular)/triangular_solve | solution.py:89
  384.4 75.9 %all-gather.5.cloned.1.call-done = f32[10240,256]{1,0:T(8,128)} async-done(((f32[640,256]{1,0:T(8,128)}), f32[10240,256]{1,0:T(8,128)}) %all-gather.5.cloned.1.call-update) | async-done | bytes 10485776 | tf_op jit(solution)/shard_map/all_gather | solution.py:121
  460.3 13.6 %gather_fusion.1 = f32[120,128,256]{2,1,0:T(8,128)} fusion(f32[80,128,256]{2,1,0:T(8,128)} %bitcast.177, s32[1024]{0:T(1024)S(1)} %pad_clamp_fusion), kind=kCustom, calls=%fused_computation.1 | custom fusion | bytes 31457760 | tf_op jit(solution)/shard_map/gather | solution.py:123
  473.9 20.2 %convolution_bitcast_fusion.2 = f32[120,128,256]{1,2,0:T(8,128)} fusion(f32[120,128,256]{2,1,0:T(8,128)} %gather_fusion.1, bf16[120,128,128]{2,1,0:T(8,128)(2,1)} %param.8), kind=kOutput, calls=%fused_computation.14 | convolution fusion | flops 6039797760 | bytes 35389440 | tf_op jit(solution)/shard_map/sij,sjk->sik/dot_general | solution.py:124
  494.1 15.6 %copy.109 = f32[120,128,256]{2,1,0:T(8,128)} copy(f32[120,128,256]{1,2,0:T(8,128)} %convolution_bitcast_fusion.2) | data formatting | bytes 31457280 | tf_op jit(solution)/shard_map/sij,sjk->sik/dot_general | solution.py:124
  509.7 17.9 %reshape.194 = f32[120,32768,1,1]{1,0,2,3:T(8,128)} reshape(f32[120,128,256]{2,1,0:T(8,128)} %copy.109) | data formatting | bytes 31457280 | tf_op jit(solution)/shard_map/reshape | solution.py:129
  527.5 16.0 %convolution_bitcast_fusion = f32[2,4,5,32768]{3,2,0,1:T(8,128)S(1)} fusion(f32[120,32768,1,1]{1,0,2,3:T(8,128)} %reshape.194, f32[120]{0:T(128)S(1)} %copy-done.3, s32[120]{0:T(128)S(1)} %copy-done.1, s32[4,2,5]{2,1,0:T(2,128)S(1)} %multiply_add_fusion), kind=kOutput, calls=%fused_computation.10 | convolution fusion | flops 1887446400 | bytes 20972640 | tf_op jit(solution)/shard_map/dot_general | solution.py:127
  570.5 47.9 %all-to-all-done.8 = f32[4,5,32768]{2,1,0:T(8,128)} async-done(((f32[4,5,32768]{2,1,0:T(8,128)}), f32[4,5,32768]{2,1,0:T(8,128)}, u32[]{:S(2)}, u32[]{:S(2)}) %all-to-all-start.8) | async-done | bytes 2621472 | tf_op jit(solution)/shard_map/all_to_all | solution.py:29
  623.1 13.0 %all_to_all.100 = f32[4,32,1024]{2,1,0:T(8,128)S(1)} all-to-all(f32[4,32,1024]{2,1,0:T(8,128)S(1)} %maximum_bitcast_fusion), channel_id=1, replica_groups=mesh['col_0'=4,'col_1'=2,'row_0'=4,'row_1'=4] {'row_1'}, dimensions={0} | all-to-all | bytes 1048576 | tf_op jit(solution)/shard_map/all_to_all | solution.py:21
  636.2 11.7 %all_to_all.101 = f32[32,1,1024]{2,1,0:T(1,128)S(1)} all-to-all(f32[32,1,1024]{2,1,0:T(1,128)S(1)} %all_to_all.67), channel_id=1, replica_groups=mesh['col_0'=4,'col_1'=2,'row_0'=4,'row_1'=4] {'col_0','col_1','row_0'}, dimensions={0} | all-to-all | bytes 262144 | tf_op jit(solution)/shard_map/all_to_all | solution.py:29
  696.7 11.7 %cholesky.265 = f32[128,128]{1,0:T(8,128)S(1)} custom-call(f32[128,128]{1,0:T(8,128)S(1)} %convolution_subtract_fusion.6), custom_call_target="Cholesky" | custom-call | tf_op jit(solution)/shard_map/jit(cholesky)/cholesky | solution.py:88
  715.1 19.8 %custom-call.20 = f32[2,128,128]{1,2,0:T(8,128)S(1)} custom-call(f32[2,128,128]{2,1,0:T(8,128)S(1)} %get-tuple-element.31), custom_call_target="InvertDiagBlocksLowerTriangular" | custom-call | tf_op jit(solution)/shard_map/jit(_solve_triangular)/triangular_solve | solution.py:89
  760.0 11.9 %cholesky.299 = f32[128,128]{1,0:T(8,128)S(1)} custom-call(f32[128,128]{1,0:T(8,128)S(1)} %convolution_subtract_fusion.5), custom_call_target="Cholesky" | custom-call | tf_op jit(solution)/shard_map/jit(cholesky)/cholesky | solution.py:88
  778.6 19.7 %custom-call.22 = f32[2,128,128]{1,2,0:T(8,128)S(1)} custom-call(f32[2,128,128]{2,1,0:T(8,128)S(1)} %get-tuple-element.32), custom_call_target="InvertDiagBlocksLowerTriangular" | custom-call | tf_op jit(solution)/shard_map/jit(_solve_triangular)/triangular_solve | solution.py:89
  866.1 11.7 %cholesky.333 = f32[128,128]{1,0:T(8,128)S(1)} custom-call(f32[128,128]{1,0:T(8,128)S(1)} %convolution_subtract_fusion.4), custom_call_target="Cholesky" | custom-call | tf_op jit(solution)/shard_map/jit(cholesky)/cholesky | solution.py:88
  884.7 20.0 %custom-call.24 = f32[2,128,128]{1,2,0:T(8,128)S(1)} custom-call(f32[2,128,128]{2,1,0:T(8,128)S(1)} %get-tuple-element.33), custom_call_target="InvertDiagBlocksLowerTriangular" | custom-call | tf_op jit(solution)/shard_map/jit(_solve_triangular)/triangular_solve | solution.py:89
  (197 shorter events, 325.2 us)
Async XLA Ops:
  7.8 165.0 %copy-start.2 = (f32[120]{0:T(128)}, f32[120]{0:T(128)S(1)}, u32[]{:S(2)}) copy-start(f32[120]{0:T(128)S(1)} %compare_convert_fusion) | copy-start | bytes 1444
  12.6 10.8 %all-to-all-start = ((f32[8,5,128]{2,1,0:T(8,128)}), f32[8,5,128]{2,1,0:T(8,128)S(1)}, u32[]{:S(2)}, u32[]{:S(2)}) async-start(f32[8,5,128]{2,1,0:T(8,128)} %fusion.51), calls=%async_computation | async-start | bytes 65536 | tf_op jit(solution)/shard_map/all_to_all | solution.py:21
  18.0 87.5 %all-gather.3.cloned.1.call-start = ((), (), s32[]{:S(2)}) async-start(), calls=%async_computation.17 | async-start | bytes 11141120 | tf_op jit(solution)/shard_map/all_gather | solution.py:121
  154.9 17.9 %copy-start.1 = (s32[120]{0:T(128)S(1)}, s32[120]{0:T(128)}, u32[]{:S(2)}) copy-start(s32[120]{0:T(128)} %param.9) | copy-start | bytes 1444
  205.8 68.0 %copy-start = (f32[640,256]{1,0:T(8,128)S(1)}, f32[640,256]{1,0:T(8,128)}, u32[]{:S(2)}) copy-start(f32[640,256]{1,0:T(8,128)} %param.12) | copy-start | bytes 1966084
  298.0 11.3 %all-to-all-start.5 = ((f32[32,2,256]{2,1,0:T(2,128)}), f32[32,2,256]{2,1,0:T(2,128)S(1)}, u32[]{:S(2)}, u32[]{:S(2)}) async-start(f32[32,2,256]{2,1,0:T(2,128)} %broadcast_in_dim.28), calls=%async_computation.5 | async-start | bytes 131072 | tf_op jit(solution)/shard_map/all_to_all | solution.py:42
  310.1 10.6 %all-to-all-start.6 = ((f32[4,32,2,256]{3,2,1,0:T(2,128)}), f32[4,32,2,256]{3,2,1,0:T(2,128)S(1)}, u32[]{:S(2)}, u32[]{:S(2)}) async-start(f32[4,32,2,256]{3,2,1,0:T(2,128)} %broadcast_in_dim.29), calls=%async_computation.6 | async-start | bytes 524288 | tf_op jit(solution)/shard_map/all_to_all | solution.py:42
  313.5 146.8 %all-gather.5.cloned.1.call-start = ((), (), s32[]{:S(2)}) async-start(), calls=%async_computation.18 | async-start | bytes 11141120 | tf_op jit(solution)/shard_map/all_gather | solution.py:121
  361.7 0.6 copy-start.4
  509.7 17.9 %copy-start.3 = (f32[120]{0:T(128)S(1)}, f32[120]{0:T(128)}, u32[]{:S(2)}) copy-start(f32[120]{0:T(128)} %copy-done.2) | copy-start | bytes 1444
  564.1 54.3 %all-to-all-start.8 = ((f32[4,5,32768]{2,1,0:T(8,128)}), f32[4,5,32768]{2,1,0:T(8,128)}, u32[]{:S(2)}, u32[]{:S(2)}) async-start(f32[4,5,32768]{2,1,0:T(8,128)} %copy.111), calls=%async_computation.8 | async-start | bytes 8388608 | tf_op jit(solution)/shard_map/all_to_all | solution.py:29
  570.3 140.7 %copy-start.5 = (s32[2,2]{1,0:T(2,128)S(1)}, s32[2,2]{1,0:T(2,128)}, u32[]{:S(2)}) copy-start(s32[2,2]{1,0:T(2,128)} %copy-done.4) | copy-start | bytes 52
  660.4 13.6 %all-to-all-start.12 = ((f32[4,32,1024]{2,1,0:T(8,128)}), f32[4,32,1024]{2,1,0:T(8,128)S(1)}, u32[]{:S(2)}, u32[]{:S(2)}) async-start(f32[4,32,1024]{2,1,0:T(8,128)} %broadcast_in_dim.31), calls=%async_computation.12 | async-start | bytes 1048576 | tf_op jit(solution)/shard_map/all_to_all | solution.py:42
  832.8 10.8 %all-to-all-start.16 = ((f32[4,32,2,256]{3,2,1,0:T(2,128)}), f32[4,32,2,256]{3,2,1,0:T(2,128)S(1)}, u32[]{:S(2)}, u32[]{:S(2)}) async-start(f32[4,32,2,256]{3,2,1,0:T(2,128)} %broadcast_in_dim.33), calls=%async_computation.16 | async-start | bytes 524288 | tf_op jit(solution)/shard_map/all_to_all | solution.py:42
Sparse Core Ops, SparseCore 0:
  25.7 79.7 all-gather.2
  384.5 75.7 all-gather.4
where the time goes:
time: 925 us; the launch traced here: 915 us
  other arithmetic  240 us (26%)
  waiting for transfers between devices  239 us (26%)
  blocking collectives  170 us (18%)
  local copies, waits for them, and re-layouts  130 us (14%)
  matrix products  89.4 us (10%)
  starting transfers between devices  24.7 us (3%)
  between operations  21.3 us (2%)
    all_gather x2, waiting for transfers between devices, body(): gathered = lax.all_gather(mapped_scaled, ROW, axis=0, tiled=True)  155 us
    another operation x27, other arithmetic, inverse_lower(): lower = jnp.linalg.cholesky(gram)  138 us
    all_to_all x4, blocking collectives, sum_in_two_steps(): lax.all_to_all(nearer, far, split_axis=0, concat_axis=0, tiled=True)  96.7 us
    another operation x9, other arithmetic, inverse_lower(): jax.scipy.linalg.solve_triangular(lower, jnp.eye(gram.shape[0], dtype=jnp...  79.3 us
    all_to_all x5, blocking collectives, sent_and_summed(): lax.all_to_all(parts, axis, split_axis=0, concat_axis=0, tiled=True)  50.9 us
    all_to_all x1, waiting for transfers between devices, sum_in_two_steps(): lax.all_to_all(nearer, far, split_axis=0, concat_axis=0, tiled=True)  47.9 us
    dot_general x2, matrix products, body(): jnp.einsum('sij,sjk->sik', squares, picked, precision=highest, preferred_...  40.3 us
    reshape x2, local copies, waits for them, and re-layouts, body(): products.reshape(slot_count, tile_size * vec_count)  35.7 us
  transfers between devices with their start and end apart: 8, of which 8 were waited for; matrix products, arithmetic and copies ran while one was open for 0% of the time, Pallas kernels for 0%

commit v1 on v0

--- a/solution.py
+++ b/solution.py
@@ -118,7 +118,9 @@
     pending = start
     for step_number in range(ITERS):
         mapped_scaled = scaling * pending
-        gathered = lax.all_gather(mapped_scaled, ROW, axis=0, tiled=True)
+        gathered = jnp.concatenate(
+            lax.all_to_all(jnp.stack([mapped_scaled] * lax.axis_size(ROW)), ROW, 0, 0), axis=0
+        )
         gathered = gathered.reshape(n_row * own_tiles, tile_size, vec_count)
         picked = gathered[tile_cols]
         products = jnp.einsum(

time: 925 us -> 1070 us (1.16)
  blocking collectives: 170 us -> 297 us
  waiting for transfers between devices: 239 us -> 266 us
  between operations: 21.3 us -> 7.95 us
    all_to_all x0 -> x1, waiting for transfers between devices: none -> 182 us  [body(): lax.all_to_all(jnp.stack([mapped_scaled] * lax.axis_size(ROW)), ROW, 0, 0)]
    all_gather x2 -> x0, waiting for transfers between devices: 155 us -> none  [body(): gathered = lax.all_gather(mapped_scaled, ROW, axis=0, tiled=True)]
    all_to_all x0 -> x1, blocking collectives: none -> 121 us  [body(): lax.all_to_all(jnp.stack([mapped_scaled] * lax.axis_size(ROW)), ROW, 0, 0)]
  transfers between devices with their start and end apart: 8 -> 7, of which waited for: 8 -> 7; matrix products, arithmetic and copies ran while one was open for 0% -> 0% of each run, Pallas kernels for 0% -> 0%
where the time goes in v1:
time: 1070 us
  blocking collectives  297 us (28%)
  waiting for transfers between devices  266 us (25%)
  other arithmetic  239 us (22%)
  local copies, waits for them, and re-layouts  136 us (13%)
  matrix products  88.6 us (8%)
  starting transfers between devices  32.5 us (3%)
    all_to_all x1, waiting for transfers between devices, body(): lax.all_to_all(jnp.stack([mapped_scaled] * lax.axis_size(ROW)), ROW, 0, 0)  182 us
    another operation x27, other arithmetic, inverse_lower(): lower = jnp.linalg.cholesky(gram)  138 us
    all_to_all x1, blocking collectives, body(): lax.all_to_all(jnp.stack([mapped_scaled] * lax.axis_size(ROW)), ROW, 0, 0)  121 us
    all_to_all x4, blocking collectives, sum_in_two_steps(): lax.all_to_all(nearer, far, split_axis=0, concat_axis=0, tiled=True)  102 us
    another operation x9, other arithmetic, inverse_lower(): jax.scipy.linalg.solve_triangular(lower, jnp.eye(gram.shape[0], dtype=jnp...  79.7 us
    all_to_all x5, blocking collectives, sent_and_summed(): lax.all_to_all(parts, axis, split_axis=0, concat_axis=0, tiled=True)  51.8 us
    all_to_all x1, waiting for transfers between devices, sum_in_two_steps(): lax.all_to_all(nearer, far, split_axis=0, concat_axis=0, tiled=True)  47.9 us
    dot_general x2, matrix products, body(): jnp.einsum('sij,sjk->sik', squares, picked, precision=highest, preferred_...  40.3 us
  transfers between devices with their start and end apart: 7, of which 7 were waited for; matrix products, arithmetic and copies ran while one was open for 0% of the time, Pallas kernels for 0%

profile of v1, /device:TPU:0, one launch (start us, length us, event | category | flops | bytes accessed | tf_op | source)
XLA Modules:
  0.0 1067.2 jit_solution(8905205009067602785)
XLA Ops:
  30.7 182.3 %all-to-all-done.1 = f32[16,640,256]{2,1,0:T(8,128)} async-done(((f32[16,640,256]{2,1,0:T(8,128)}), f32[16,640,256]{2,1,0:T(8,128)}, u32[]{:S(2)}, u32[]{:S(2)}) %all-to-all-start.1) | async-done | bytes 10485792 | tf_op jit(solution)/shard_map/all_to_all | solution.py:122
  213.0 13.6 %gather_fusion = f32[120,128,256]{2,1,0:T(8,128)} fusion(f32[80,128,256]{2,1,0:T(8,128)} %bitcast.3, s32[1024]{0:T(1024)S(1)} %pad_clamp_fusion), kind=kCustom, calls=%fused_computation | custom fusion | bytes 31457760 | tf_op jit(solution)/shard_map/gather | solution.py:125
  226.6 20.2 %convolution_bitcast_fusion.3 = f32[120,128,256]{1,2,0:T(8,128)} fusion(f32[120,128,256]{2,1,0:T(8,128)} %gather_fusion, bf16[120,128,128]{2,1,0:T(8,128)(2,1)} %param.8), kind=kOutput, calls=%fused_computation.15 | convolution fusion | flops 6039797760 | bytes 35389440 | tf_op jit(solution)/shard_map/sij,sjk->sik/dot_general | solution.py:126
  246.8 15.6 %copy.101 = f32[120,128,256]{2,1,0:T(8,128)} copy(f32[120,128,256]{1,2,0:T(8,128)} %convolution_bitcast_fusion.3) | data formatting | bytes 31457280 | tf_op jit(solution)/shard_map/sij,sjk->sik/dot_general | solution.py:126
  262.4 17.9 %reshape.189 = f32[120,32768,1,1]{1,0,2,3:T(8,128)} reshape(f32[120,128,256]{2,1,0:T(8,128)} %copy.101) | data formatting | bytes 31457280 | tf_op jit(solution)/shard_map/reshape | solution.py:131
  280.3 16.2 %convolution_bitcast_fusion.1 = f32[2,4,5,32768]{3,2,0,1:T(8,128)S(1)} fusion(f32[120,32768,1,1]{1,0,2,3:T(8,128)} %reshape.189, f32[120]{0:T(128)S(1)} %compare_convert_fusion, s32[120]{0:T(128)S(1)} %copy-done.1, s32[4,2,5]{2,1,0:T(2,128)S(1)} %multiply_add_fusion), kind=kOutput, calls=%fused_computation.11 | convolution fusion | flops 1887446400 | bytes 20972640 | tf_op jit(solution)/shard_map/dot_general | solution.py:129
  315.0 62.9 %all_to_all.107 = f32[4,5,32768]{2,1,0:T(8,128)} all-to-all(f32[4,5,32768]{2,1,0:T(8,128)S(1)} %copy.103), channel_id=1, replica_groups=mesh['col_0'=4,'col_1'=2,'row_0'=4,'row_1'=4] {'col_0'}, dimensions={0} | all-to-all | bytes 5242880 | tf_op jit(solution)/shard_map/all_to_all | solution.py:29
  382.5 12.9 %all_to_all.108 = f32[4,32,2,256]{3,2,1,0:T(2,128)S(1)} all-to-all(f32[4,32,2,256]{3,2,1,0:T(2,128)S(1)} %bitcast.181), channel_id=1, replica_groups=mesh['col_0'=4,'col_1'=2,'row_0'=4,'row_1'=4] {'row_1'}, dimensions={0} | all-to-all | bytes 524288 | tf_op jit(solution)/shard_map/all_to_all | solution.py:21
  395.5 17.6 %all_to_all.109 = f32[32,2,256]{2,1,0:T(2,128)S(1)} all-to-all(f32[32,2,256]{2,1,0:T(2,128)S(1)} %reduce_sum.112), channel_id=1, replica_groups=mesh['col_0'=4,'col_1'=2,'row_0'=4,'row_1'=4] {'col_0','col_1','row_0'}, dimensions={0} | all-to-all | bytes 131072 | tf_op jit(solution)/shard_map/all_to_all | solution.py:29
  459.0 11.7 %cholesky.231 = f32[128,128]{1,0:T(8,128)S(1)} custom-call(f32[128,128]{1,0:T(8,128)S(1)} %convolution_subtract_fusion.7), custom_call_target="Cholesky" | custom-call | tf_op jit(solution)/shard_map/jit(cholesky)/cholesky | solution.py:88
  477.7 20.1 %custom-call.18 = f32[2,128,128]{1,2,0:T(8,128)S(1)} custom-call(f32[2,128,128]{2,1,0:T(8,128)S(1)} %get-tuple-element.30), custom_call_target="InvertDiagBlocksLowerTriangular" | custom-call | tf_op jit(solution)/shard_map/jit(_solve_triangular)/triangular_solve | solution.py:89
  500.4 121.2 %all_to_all.110 = f32[16,640,256]{2,1,0:T(8,128)} all-to-all(f32[16,640,256]{2,1,0:T(8,128)S(1)} %stack.11), channel_id=1, replica_groups=mesh['col_0'=4,'col_1'=2,'row_0'=4,'row_1'=4] {'row_0','row_1'}, dimensions={0} | all-to-all | bytes 20971520 | tf_op jit(solution)/shard_map/all_to_all | solution.py:122
  621.5 13.6 %gather_fusion.1 = f32[120,128,256]{2,1,0:T(8,128)} fusion(f32[80,128,256]{2,1,0:T(8,128)} %bitcast.175, s32[1024]{0:T(1024)S(1)} %pad_clamp_fusion), kind=kCustom, calls=%fused_computation.1 | custom fusion | bytes 31457760 | tf_op jit(solution)/shard_map/gather | solution.py:125
  635.2 20.2 %convolution_bitcast_fusion.2 = f32[120,128,256]{1,2,0:T(8,128)} fusion(f32[120,128,256]{2,1,0:T(8,128)} %gather_fusion.1, bf16[120,128,128]{2,1,0:T(8,128)(2,1)} %param.8), kind=kOutput, calls=%fused_computation.14 | convolution fusion | flops 6039797760 | bytes 35389440 | tf_op jit(solution)/shard_map/sij,sjk->sik/dot_general | solution.py:126
  655.3 15.6 %copy.109 = f32[120,128,256]{2,1,0:T(8,128)} copy(f32[120,128,256]{1,2,0:T(8,128)} %convolution_bitcast_fusion.2) | data formatting | bytes 31457280 | tf_op jit(solution)/shard_map/sij,sjk->sik/dot_general | solution.py:126
  671.0 17.9 %reshape.190 = f32[120,32768,1,1]{1,0,2,3:T(8,128)} reshape(f32[120,128,256]{2,1,0:T(8,128)} %copy.109) | data formatting | bytes 31457280 | tf_op jit(solution)/shard_map/reshape | solution.py:131
  688.8 16.0 %convolution_bitcast_fusion = f32[2,4,5,32768]{3,2,0,1:T(8,128)S(1)} fusion(f32[120,32768,1,1]{1,0,2,3:T(8,128)} %reshape.190, f32[120]{0:T(128)S(1)} %copy-done.3, s32[120]{0:T(128)S(1)} %copy-done.1, s32[4,2,5]{2,1,0:T(2,128)S(1)} %multiply_add_fusion), kind=kOutput, calls=%fused_computation.10 | convolution fusion | flops 1887446400 | bytes 20972640 | tf_op jit(solution)/shard_map/dot_general | solution.py:129
  732.2 47.9 %all-to-all-done.10 = f32[4,5,32768]{2,1,0:T(8,128)} async-done(((f32[4,5,32768]{2,1,0:T(8,128)}), f32[4,5,32768]{2,1,0:T(8,128)}, u32[]{:S(2)}, u32[]{:S(2)}) %all-to-all-start.10) | async-done | bytes 2621472 | tf_op jit(solution)/shard_map/all_to_all | solution.py:29
  856.2 11.7 %cholesky.265 = f32[128,128]{1,0:T(8,128)S(1)} custom-call(f32[128,128]{1,0:T(8,128)S(1)} %convolution_subtract_fusion.6), custom_call_target="Cholesky" | custom-call | tf_op jit(solution)/shard_map/jit(cholesky)/cholesky | solution.py:88
  874.6 19.8 %custom-call.20 = f32[2,128,128]{1,2,0:T(8,128)S(1)} custom-call(f32[2,128,128]{2,1,0:T(8,128)S(1)} %get-tuple-element.31), custom_call_target="InvertDiagBlocksLowerTriangular" | custom-call | tf_op jit(solution)/shard_map/jit(_solve_triangular)/triangular_solve | solution.py:89
  919.5 11.9 %cholesky.299 = f32[128,128]{1,0:T(8,128)S(1)} custom-call(f32[128,128]{1,0:T(8,128)S(1)} %convolution_subtract_fusion.5), custom_call_target="Cholesky" | custom-call | tf_op jit(solution)/shard_map/jit(cholesky)/cholesky | solution.py:88
  938.1 19.7 %custom-call.22 = f32[2,128,128]{1,2,0:T(8,128)S(1)} custom-call(f32[2,128,128]{2,1,0:T(8,128)S(1)} %get-tuple-element.32), custom_call_target="InvertDiagBlocksLowerTriangular" | custom-call | tf_op jit(solution)/shard_map/jit(_solve_triangular)/triangular_solve | solution.py:89
  1025.6 11.7 %cholesky.333 = f32[128,128]{1,0:T(8,128)S(1)} custom-call(f32[128,128]{1,0:T(8,128)S(1)} %convolution_subtract_fusion.4), custom_call_target="Cholesky" | custom-call | tf_op jit(solution)/shard_map/jit(cholesky)/cholesky | solution.py:88
  1044.2 20.0 %custom-call.24 = f32[2,128,128]{1,2,0:T(8,128)S(1)} custom-call(f32[2,128,128]{2,1,0:T(8,128)S(1)} %get-tuple-element.33), custom_call_target="InvertDiagBlocksLowerTriangular" | custom-call | tf_op jit(solution)/shard_map/jit(_solve_triangular)/triangular_solve | solution.py:89
  (198 shorter events, 337.1 us)
Async XLA Ops:
  1.3 279.0 %copy-start.2 = (f32[120]{0:T(128)}, f32[120]{0:T(128)S(1)}, u32[]{:S(2)}) copy-start(f32[120]{0:T(128)S(1)} %compare_convert_fusion) | copy-start | bytes 1444
  6.1 10.8 %all-to-all-start = ((f32[8,5,128]{2,1,0:T(8,128)}), f32[8,5,128]{2,1,0:T(8,128)S(1)}, u32[]{:S(2)}, u32[]{:S(2)}) async-start(f32[8,5,128]{2,1,0:T(8,128)} %fusion.51), calls=%async_computation | async-start | bytes 65536 | tf_op jit(solution)/shard_map/all_to_all | solution.py:21
  23.2 7.5 copy-start.4
  23.2 189.8 %all-to-all-start.1 = ((f32[16,640,256]{2,1,0:T(8,128)}), f32[16,640,256]{2,1,0:T(8,128)}, u32[]{:S(2)}, u32[]{:S(2)}) async-start(f32[16,640,256]{2,1,0:T(8,128)} %stack.10), calls=%async_computation.1 | async-start | bytes 20971520 | tf_op jit(solution)/shard_map/all_to_all | solution.py:122
  262.4 17.9 %copy-start.1 = (s32[120]{0:T(128)S(1)}, s32[120]{0:T(128)}, u32[]{:S(2)}) copy-start(s32[120]{0:T(128)} %param.9) | copy-start | bytes 1444
  313.4 67.5 %copy-start = (f32[640,256]{1,0:T(8,128)S(1)}, f32[640,256]{1,0:T(8,128)}, u32[]{:S(2)}) copy-start(f32[640,256]{1,0:T(8,128)} %param.12) | copy-start | bytes 1966084
  413.9 11.3 %all-to-all-start.6 = ((f32[32,2,256]{2,1,0:T(2,128)}), f32[32,2,256]{2,1,0:T(2,128)S(1)}, u32[]{:S(2)}, u32[]{:S(2)}) async-start(f32[32,2,256]{2,1,0:T(2,128)} %broadcast_in_dim.28), calls=%async_computation.6 | async-start | bytes 131072 | tf_op jit(solution)/shard_map/all_to_all | solution.py:42
  425.9 10.6 all-to-all-start.7
  477.1 0.6 copy-start.5
  671.0 17.9 %copy-start.3 = (f32[120]{0:T(128)S(1)}, f32[120]{0:T(128)}, u32[]{:S(2)}) copy-start(f32[120]{0:T(128)} %copy-done.2) | copy-start | bytes 1444
  725.3 54.7 %all-to-all-start.10 = ((f32[4,5,32768]{2,1,0:T(8,128)}), f32[4,5,32768]{2,1,0:T(8,128)}, u32[]{:S(2)}, u32[]{:S(2)}) async-start(f32[4,5,32768]{2,1,0:T(8,128)} %copy.111), calls=%async_computation.10 | async-start | bytes 8388608 | tf_op jit(solution)/shard_map/all_to_all | solution.py:29
  732.0 138.6 %copy-start.6 = (s32[2,2]{1,0:T(2,128)S(1)}, s32[2,2]{1,0:T(2,128)}, u32[]{:S(2)}) copy-start(s32[2,2]{1,0:T(2,128)} %copy-done.5) | copy-start | bytes 52
  819.9 13.6 %all-to-all-start.14 = ((f32[4,32,1024]{2,1,0:T(8,128)}), f32[4,32,1024]{2,1,0:T(8,128)S(1)}, u32[]{:S(2)}, u32[]{:S(2)}) async-start(f32[4,32,1024]{2,1,0:T(8,128)} %broadcast_in_dim.31), calls=%async_computation.14 | async-start | bytes 1048576 | tf_op jit(solution)/shard_map/all_to_all | solution.py:42
  992.3 10.8 %all-to-all-start.18 = ((f32[4,32,2,256]{3,2,1,0:T(2,128)}), f32[4,32,2,256]{3,2,1,0:T(2,128)S(1)}, u32[]{:S(2)}, u32[]{:S(2)}) async-start(f32[4,32,2,256]{3,2,1,0:T(2,128)} %broadcast_in_dim.33), calls=%async_computation.18 | async-start | bytes 524288 | tf_op jit(solution)/shard_map/all_to_all | solution.py:42
